TPU v7x, 32 devices: a whole 2x2x4 slice. The times are simulated.
32 devices in a mesh: sample: 4 (over x, core), gene: 2 (over y), cohort: 4 (over z).
Axes of the slice: x: 2, y: 2, z: 4, core: 2. Of those that a mesh axis runs over, the one named last changes fastest.
Arguments:
- dosage: bfloat16 [8192, 16384], P(('sample', 'cohort'), 'gene'), may hold values from 0 to 2
- covariates: bfloat16 [8192, 32], P(('sample', 'cohort')), may hold values from 0 to 2
- phenotype: bfloat16 [8192], P(('sample', 'cohort')), may hold values from -6 to 6
- sample_mask: int32 [8192], P(('sample', 'cohort')), may hold values 0 or 1
- variant_weight: float32 [16384], replicated, may hold values from 0.1 to 1
- bucket_owner: int32 [128], replicated, may hold values from 0 to 7, as said below
- variant_gene: int32 [16384], replicated, may hold values from -1 to 63, as said below
Outputs:
- gram_tiles: float32 [8, 16, 128, 128], P(('gene', 'cohort'), 'sample')
- rho_stats: float32 [8, 64], P(None, ('gene', 'cohort'))
- gene_trace: float32 [64], P(('gene', 'cohort'))
Inputs may be any that keep to these rules, and one draw needn't show every extreme that they name: `bucket_owner`: every owner holds exactly 16 buckets, at most 8 of them among the 64 buckets of one index of gene, and some owner exactly 8; of the buckets of one index of gene, exactly 16 belong to owners whose index leaves a given remainder on division by the size of the cohort axis. `variant_gene`: genes o * 8 to (o + 1) * 8 - 1 lie in the buckets of owner o, each in one or more whole buckets that are consecutive among that owner's buckets; all its buckets are full but its last, whose first 10 to 128 columns are live and the rest -1.
All inputs are finite; a program needn't handle non-finite values. No bound on the sum of `sample_mask` on one device may be relied on, other than what follows from the above.
Results may differ from a plain program's by a relative error of at most 0.0003.
Values may be sent and summed in bfloat16 or wider, within the bound.
A program may use at most 128 MiB of HBM per device.

v0:
```python
import math

import jax
import jax.numpy as jnp
from jax import lax
from jax.sharding import PartitionSpec as P

BUCKET_WIDTH = 128
GENES_OWN = 8


RHO_GRID = (0.0, 0.01, 0.04, 0.09, 0.16, 0.25, 0.5, 1.0)


def solve_moments(factor, rhs):
    half = lax.linalg.triangular_solve(factor, rhs, left_side=True, lower=True)
    return lax.linalg.triangular_solve(factor, half, left_side=True, lower=True, transpose_a=True)


def inner_rows(first, second):
    return lax.dot_general(
        first, second, (((0,), (0,)), ((), ())), preferred_element_type=jnp.float32
    )


def block_rank(labels, group_count, label_count):
    onehot = (labels[:, None] == jnp.arange(label_count, dtype=jnp.int32)[None, :]).astype(
        jnp.int32
    )
    blocks = onehot.reshape(group_count, labels.shape[0] // group_count, label_count)
    return jnp.sum((jnp.cumsum(blocks, axis=1) - blocks) * blocks, axis=2).reshape(labels.shape[0])


def finish_slots(
    gram, cross, slot_bucket, moments, variant_weight, variant_gene, owner_here, sample_total
):
    cov_count = moments.shape[0]
    slot_count = gram.shape[0]
    span_width = gram.shape[1]
    factor = jnp.linalg.cholesky(moments[:, :cov_count])
    beta_hat = solve_moments(factor, moments[:, cov_count:])[:, 0]
    cov_cross = cross[:, :cov_count, :]
    raw_score = cross[:, cov_count, :]
    stacked = jnp.transpose(cov_cross, (1, 0, 2)).reshape(cov_count, slot_count * span_width)
    solved = solve_moments(factor, stacked).reshape(cov_count, slot_count, span_width)
    projected = jnp.einsum("bcj,cbk->bjk", cov_cross, solved, precision=lax.Precision.HIGHEST)
    scores = raw_score - jnp.einsum(
        "bcj,c->bj", cov_cross, beta_hat, precision=lax.Precision.HIGHEST
    )
    bucket_total = variant_gene.shape[0] // span_width
    weight_rows = jnp.where(variant_gene >= 0, variant_weight, 0.0).reshape(
        bucket_total, span_width
    )
    live_weight = jnp.take(weight_rows, slot_bucket, axis=0)
    tiles = live_weight[:, :, None] * live_weight[:, None, :] * (gram - projected) / sample_total
    zscore = (live_weight * scores / math.sqrt(sample_total)).reshape(slot_count * span_width)
    gene_rows = (
        jnp.take(variant_gene.reshape(bucket_total, span_width), slot_bucket, axis=0)
        - owner_here * GENES_OWN
    )
    member = (
        gene_rows.reshape(slot_count * span_width)[:, None]
        == jnp.arange(GENES_OWN, dtype=jnp.int32)[None, :]
    ).astype(jnp.float32)
    squares = jnp.dot(zscore * zscore, member, precision=lax.Precision.HIGHEST)
    burden_sum = jnp.dot(zscore, member, precision=lax.Precision.HIGHEST)
    diagonal = jnp.diagonal(tiles, axis1=1, axis2=2).reshape(slot_count * span_width)
    trace_sum = jnp.dot(diagonal, member, precision=lax.Precision.HIGHEST)
    return (tiles, squares, burden_sum, trace_sum)


def shards(dosage, covariates, phenotype, sample_mask, variant_weight, bucket_owner, variant_gene):
    gene_count = lax.axis_size("gene")
    cohort_count = lax.axis_size("cohort")
    sample_count = lax.axis_size("sample")
    owner_count = gene_count * cohort_count
    span_width = BUCKET_WIDTH
    sample_rows = dosage.shape[0]
    src_buckets = dosage.shape[1] // span_width
    total_buckets = bucket_owner.shape[0]
    held_slots = total_buckets // owner_count
    cap_slots = held_slots // 2
    share = held_slots // sample_count
    sample_total = sample_rows * sample_count * cohort_count
    cohort_here = lax.axis_index("cohort")
    owner_here = lax.axis_index("gene") * cohort_count + cohort_here
    sample_keep = sample_mask.astype(jnp.bfloat16)
    masked_cov = covariates * sample_keep[:, None]
    left_cols = jnp.concatenate([masked_cov, (phenotype * sample_keep)[:, None]], axis=1)
    moments = lax.psum(
        inner_rows(masked_cov, jnp.concatenate([covariates, phenotype[:, None]], axis=1)),
        ("sample", "cohort"),
    )
    masked_dosage = (dosage * sample_keep[:, None]).reshape(sample_rows, src_buckets, span_width)
    owner_ids = jnp.arange(owner_count, dtype=jnp.int32)
    onehot = (bucket_owner[:, None] == owner_ids[None, :]).astype(jnp.int32)
    owner_rank = jnp.sum((jnp.cumsum(onehot, axis=0) - onehot) * onehot, axis=1)
    pair_rank = block_rank(bucket_owner, gene_count, owner_count)
    source_start = lax.axis_index("gene") * src_buckets
    mine_owner = lax.dynamic_slice_in_dim(bucket_owner, source_start, src_buckets)
    mine_rank = lax.dynamic_slice_in_dim(pair_rank, source_start, src_buckets)
    own_key = jnp.where(bucket_owner == owner_here, owner_rank, held_slots)
    own_bucket = (
        jnp.zeros((held_slots,), jnp.int32)
        .at[own_key]
        .set(jnp.arange(total_buckets, dtype=jnp.int32), mode="drop")
    )
    own_source = own_bucket // src_buckets
    own_pair = jnp.take(pair_rank, own_bucket)
    cohort_ids = jnp.arange(cohort_count, dtype=jnp.int32)
    flat_index = (
        (own_source[None, :] * cohort_count + cohort_ids[:, None]) * cap_slots + own_pair[None, :]
    ).reshape(cohort_count * held_slots)
    send_from = (
        jnp.full((owner_count * cap_slots,), -1, jnp.int32)
        .at[mine_owner * cap_slots + mine_rank]
        .set(jnp.arange(src_buckets, dtype=jnp.int32))
    )
    send_pick = jnp.maximum(send_from, 0)
    cohort_left = lax.all_gather(left_cols[:, None, :], "cohort", axis=1, tiled=True)
    packed = (
        jnp.take(masked_dosage, send_pick, axis=1)
        * (send_from >= 0).astype(jnp.bfloat16)[None, :, None]
    )
    packed = packed.reshape(sample_rows, owner_count, cap_slots, span_width)
    arrived = lax.all_to_all(packed, ("gene", "cohort"), split_axis=1, concat_axis=1, tiled=True)
    arrived = arrived.reshape(sample_rows, owner_count * cap_slots, span_width)
    owned = jnp.take(arrived, flat_index, axis=1).reshape(
        sample_rows, cohort_count, held_slots, span_width
    )
    gram = jnp.einsum("schj,schk->hjk", owned, owned, preferred_element_type=jnp.float32)
    cross = jnp.einsum("sci,schk->hik", cohort_left, owned, preferred_element_type=jnp.float32)
    slot_start = lax.axis_index("sample") * share
    gram, cross = lax.psum((gram, cross), "sample")
    tiles, squares, burden_sum, trace_sum = finish_slots(
        gram, cross, own_bucket, moments, variant_weight, variant_gene, owner_here, sample_total
    )
    tiles = lax.dynamic_slice_in_dim(tiles, slot_start, share)
    rho_col = jnp.array(RHO_GRID, dtype=jnp.float32)[:, None]
    rho_stats = (
        (1.0 - rho_col) * squares[None, :] + rho_col * (burden_sum * burden_sum)[None, :]
    ) / span_width
    gene_trace = trace_sum / span_width
    return (tiles[None], rho_stats, gene_trace)


def solution(mesh):
    placed = (
        P(("sample", "cohort"), "gene"),
        P(("sample", "cohort"), None),
        P(("sample", "cohort")),
        P(("sample", "cohort")),
        P(),
        P(),
        P(),
    )
    return jax.shard_map(
        shards,
        mesh=mesh,
        in_specs=placed,
        out_specs=(
            P(("gene", "cohort"), "sample", None, None),
            P(None, ("gene", "cohort")),
            P(("gene", "cohort")),
        ),
        check_vma=False,
    )
```

profile of v0, /device:TPU:0, one launch (start us, length us, event | category | flops | bytes accessed | tf_op | source)
XLA Modules:
  0.0 415.0 jit_solution(13362130793251348657)
XLA Ops:
  7.2 0.7 eq.53
  8.4 0.7 compare_select_fusion.1
  9.1 0.8 scatter_custom_fusion.1
  9.9 11.9 %copy.49 = bf16[512,8192]{0,1:T(8,128)(2,1)} copy(bf16[512,8192]{1,0:T(8,128)(2,1)} %param.10) | data formatting | bytes 16777216 | tf_op args[0]
  21.9 7.1 %broadcast_multiply_fusion = bf16[512,8192]{0,1:T(8,128)(2,1)} fusion(bf16[512,8192]{0,1:T(8,128)(2,1)} %copy.49, bf16[512]{0:T(512)(128)(2,1)S(1)} %get-tuple-element.10), kind=kLoop, calls=%fused_computation.12 | loop fusion | flops 4194304 | bytes 16778240 | tf_op jit(solution)/shard_map/mul | solution.py:94
  29.0 11.9 %copy.50 = bf16[512,64,128]{2,0,1:T(8,128)(2,1)} copy(bf16[512,64,128]{0,2,1:T(8,128)(2,1)} %bitcast.117) | data formatting | bytes 16777216 | tf_op jit(solution)/shard_map/reshape | solution.py:94
  40.9 8.9 %gather_fusion.4 = bf16[64,512,128]{2,1,0:T(8,128)(2,1)} fusion(bf16[512,64,128]{2,0,1:T(8,128)(2,1)} %copy.50, s32[1024]{0:T(1024)S(1)} %pad_clamp_fusion.1), kind=kCustom, calls=%fused_computation.clone | custom fusion | bytes 16777472 | tf_op jit(solution)/shard_map/jit(_take)/gather | solution.py:122
  49.8 7.5 %bitcast_multiply_fusion = bf16[512,64,128]{2,0,1:T(8,128)(2,1)} fusion(bf16[64,512,128]{2,1,0:T(8,128)(2,1)} %gather_fusion.4, pred[64]{0:T(512)(128)(4,1)S(1)} %get-tuple-element.15, bf16[64]{0:T(256)(128)(2,1)S(1)} %get-tuple-element.14), kind=kLoop, calls=%fused_computation.10 | loop fusion | flops 8388608 | bytes 16777408 | tf_op jit(solution)/shard_map/mul | solution.py:122
  57.3 7.4 %all-to-all-start = ((bf16[512,8,8,128]{3,0,2,1:T(8,128)(2,1)}), bf16[512,8,8,128]{3,0,2,1:T(8,128)(2,1)}, u32[]{:S(2)}, u32[]{:S(2)}) async-start(bf16[512,8,8,128]{3,0,2,1:T(8,128)(2,1)} %bitcast.116), calls=%async_computation | async-start | bytes 16777216 | tf_op jit(solution)/shard_map/all_to_all | solution.py:126
  65.3 1.0 scatter_custom_fusion
  66.3 0.7 gather_fusion.1
  67.1 187.3 %all-gather.1 = bf16[4,33,512]{2,1,0:T(8,128)(2,1)S(1)} all-gather(bf16[1,33,512]{2,1,0:T(8,128)(2,1)S(1)} %maximum_bitcast_fusion), channel_id=2, replica_groups=mesh['sample'=4,'gene'=2,'cohort'=4] {'cohort'}, dimensions={0}, use_global_device_ids=true | all-gather | bytes 168960 | tf_op jit(solution)/shard_map/all_gather | solution.py:120
  254.6 58.5 %psum.23 = f32[32,33]{0,1:T(8,128)S(1)} all-reduce(f32[32,33]{0,1:T(8,128)S(1)} %fusion.21), channel_id=1, replica_groups=mesh['sample'=4,'gene'=2,'cohort'=4] {'sample','cohort'}, use_global_device_ids=true, to_apply=%region_8.10 | all-reduce | flops 1056 | bytes 8448 | tf_op jit(solution)/shard_map/psum | solution.py:90
  313.2 2.9 cholesky.16
  316.1 0.6 compare_reduce_fusion
  316.8 0.7 fusion.25
  317.4 2.4 custom-call.12
  321.1 8.9 %gather_fusion.5 = bf16[64,512,128]{2,1,0:T(8,128)(2,1)} fusion(bf16[512,64,128]{2,0,1:T(8,128)(2,1)} %bitcast.4, s32[1024]{0:T(1024)S(1)} %pad_clamp_fusion), kind=kCustom, calls=%fused_computation.1.clone | custom fusion | bytes 16777472 | tf_op jit(solution)/shard_map/jit(_take)/gather | solution.py:128
  330.0 7.5 %broadcast_select_fusion = bf16[64,512,128]{2,1,0:T(8,128)(2,1)} fusion(bf16[64,512,128]{2,1,0:T(8,128)(2,1)} %gather_fusion.5, pred[64]{0:T(512)(128)(4,1)S(1)} %compare_and_fusion), kind=kLoop, calls=%fused_computation.11 | loop fusion | flops 4194304 | bytes 16777280 | tf_op jit(solution)/shard_map/jit(_take)/select_n | solution.py:128
  337.5 9.2 %fusion.2 = f32[16,128,128]{2,1,0:T(8,128)} fusion(bf16[512,4,16,128]{3,0,2,1:T(8,128)(2,1)} %bitcast.114), kind=kOutput, calls=%fused_computation.13 | convolution fusion | flops 1073741824 | bytes 9437184 | tf_op jit(solution)/shard_map/schj,schk->hjk/dot_general | solution.py:131
  346.7 5.6 %convolution_bitcast_fusion = f32[16,33,128]{2,1,0:T(8,128)} fusion(bf16[512,4,16,128]{3,0,2,1:T(8,128)(2,1)} %bitcast.115, bf16[512,4,33,1]{0,2,1,3:T(8,128)(2,1)S(1)} %reshape.236), kind=kOutput, calls=%fused_computation.17 | convolution fusion | flops 276824064 | bytes 8794112 | tf_op jit(solution)/shard_map/sci,schk->hik/dot_general | solution.py:132
  352.7 38.1 %all-reduce.3.cloned.1.call-done = (f32[16,128,128]{2,1,0:T(8,128)}, f32[16,33,128]{2,1,0:T(8,128)}) async-done(((f32[16,128,128]{2,1,0:T(8,128)}, f32[16,33,128]{2,1,0:T(8,128)}), (f32[16,128,128]{2,1,0:T(8,128)}, f32[16,33,128]{2,1,0:T(8,128)})) %all-reduce.3.cloned.1.call-update) | async-done | bytes 1318928 | tf_op jit(solution)/shard_map/psum | solution.py:134
  390.8 0.8 slice.50
  391.6 1.4 fusion.12
  393.0 1.2 fusion.15
  394.7 3.3 fusion.6
  398.0 4.6 %copy.60 = f32[16,128,128]{0,2,1:T(8,128)} copy(f32[16,128,128]{2,1,0:T(8,128)S(1)} %fusion.6) | data formatting | bytes 2097152 | tf_op jit(solution)/shard_map/div | solution.py:55
  402.6 1.8 gather_fusion.3
  404.4 1.1 fusion.7
  406.1 0.6 fusion.8
  406.7 0.7 dynamic-slice_bitcast_fusion
  407.5 0.7 add_multiply_fusion
  (63 shorter events, 4.0 us)
Async XLA Ops:
  9.9 12.0 %copy-start.4 = (bf16[512]{0:T(512)(128)(2,1)S(1)}, bf16[512]{0:T(512)(128)(2,1)}, u32[]{:S(2)}) copy-start(bf16[512]{0:T(512)(128)(2,1)} %param.12) | copy-start | bytes 3076
  9.9 11.9 %copy-start.5 = (s32[512]{0:T(512)S(1)}, s32[512]{0:T(512)}, u32[]{:S(2)}) copy-start(s32[512]{0:T(512)} %param.13) | copy-start | bytes 6148
  57.3 7.5 %copy-start.3 = (s32[128]{0:T(128)S(1)}, s32[128]{0:T(128)}, u32[]{:S(2)}) copy-start(s32[128]{0:T(128)} %param.15) | copy-start | bytes 1540
  57.3 9.8 %copy-start.2 = (bf16[512,32]{0,1:T(8,128)(2,1)S(1)}, bf16[512,32]{0,1:T(8,128)(2,1)}, u32[]{:S(2)}) copy-start(bf16[512,32]{0,1:T(8,128)(2,1)} %param.11) | copy-start | bytes 98308
  57.3 262.5 %copy-start = (s32[16384]{0:T(1024)S(1)}, s32[16384]{0:T(1024)}, u32[]{:S(2)}) copy-start(s32[16384]{0:T(1024)} %param.16) | copy-start | bytes 196612
  57.3 262.5 %copy-start.1 = (f32[16384]{0:T(1024)S(1)}, f32[16384]{0:T(1024)}, u32[]{:S(2)}) copy-start(f32[16384]{0:T(1024)} %param.14) | copy-start | bytes 196612
  57.3 263.7 %all-to-all-start = ((bf16[512,8,8,128]{3,0,2,1:T(8,128)(2,1)}), bf16[512,8,8,128]{3,0,2,1:T(8,128)(2,1)}, u32[]{:S(2)}, u32[]{:S(2)}) async-start(bf16[512,8,8,128]{3,0,2,1:T(8,128)(2,1)} %bitcast.116), calls=%async_computation | async-start | bytes 16777216 | tf_op jit(solution)/shard_map/all_to_all | solution.py:126
  64.8 326.0 %all-reduce.3.cloned.1.call-start = ((), (), s32[]{:S(2)}) async-start(), calls=%async_computation.1 | async-start | bytes 2752512 | tf_op jit(solution)/shard_map/psum | solution.py:134
  352.3 55.2 %copy-start.6 = (f32[8]{0:T(128)S(1)}, f32[8]{0:T(128)}, u32[]{:S(2)}) copy-start(f32[8]{0:T(128)} %constant.178.clone) | copy-start | bytes 100
  352.3 55.2 %copy-start.7 = (f32[8]{0:T(128)S(1)}, f32[8]{0:T(128)}, u32[]{:S(2)}) copy-start(f32[8]{0:T(128)} %constant.180) | copy-start | bytes 100
Sparse Core Ops, SparseCore 0:
  352.5 38.2 all-reduce.2
where the time goes:
time: 416 us; the launch traced here: 415 us
  blocking collectives  246 us (59%)
  local copies, waits for them, and re-layouts  54.4 us (13%)
  waiting for transfers between devices  38.1 us (9%)
  other arithmetic  31.2 us (8%)
  matrix products  23.8 us (6%)
  between operations  14.3 us (3%)
  starting transfers between devices  7.46 us (2%)
    all_gather x1, blocking collectives, shards(): lax.all_gather(left_cols[:, None, :], 'cohort', axis=1, tiled=True)  187 us
    psum x1, blocking collectives, shards(): lax.psum(inner_rows(masked_cov, jnp.concatenate([covariates, phenotype[:,...  58.5 us
    psum x1, waiting for transfers between devices, shards(): gram, cross = lax.psum((gram, cross), 'sample')  38.1 us
    unnamed x18, local copies, waits for them, and re-layouts  12 us
    reshape x1, local copies, waits for them, and re-layouts, shards(): (dosage * sample_keep[:, None]).reshape(sample_rows, src_buckets, span_wi...  11.9 us
    dot_general x1, matrix products, shards(): jnp.einsum('schj,schk->hjk', owned, owned, preferred_element_type=jnp.flo...  9.24 us
    gather x1, local copies, waits for them, and re-layouts, shards(): jnp.take(arrived, flat_index, axis=1)  8.91 us
    gather x1, local copies, waits for them, and re-layouts, shards(): jnp.take(masked_dosage, send_pick, axis=1)  8.9 us
  transfers between devices with their start and end apart: 2, of which 1 were waited for; matrix products, arithmetic and copies ran while one was open for 3% of the time, Pallas kernels for 0%

commit v1 on v0

--- a/solution.py
+++ b/solution.py
@@ -1,8 +1,11 @@
+import functools
 import math
 
 import jax
 import jax.numpy as jnp
 from jax import lax
+from jax.experimental import pallas as pl
+from jax.experimental.pallas import tpu as pltpu
 from jax.sharding import PartitionSpec as P
 
 BUCKET_WIDTH = 128
@@ -144,6 +147,373 @@
     return (tiles[None], rho_stats, gene_trace)
 
 
+UNIT = 200
+
+
+def contract_rows(first, second):
+    return lax.dot_general(
+        first, second, (((0,), (0,)), ((), ())), preferred_element_type=jnp.float32
+    )
+
+
+def square_iota():
+    shape = (BUCKET_WIDTH, BUCKET_WIDTH)
+    return (
+        lax.broadcasted_iota(jnp.int32, shape, 0),
+        lax.broadcasted_iota(jnp.int32, shape, 1),
+    )
+
+
+def window_kernel(
+    covs, sample_total, order_ref, dosage_ref, side_ref, weight_ref, gene_ref,
+    tile_ref, rho_ref, trace_ref,
+    panel_ref, left_t, own, give, take_core, take_x, take_near, take_far, final, mom_out, mom_in, stats,
+    core_send, core_recv, x_send, x_recv, near_send, near_recv, far_send, far_recv,
+    swap_send, swap_recv, mom_send, mom_recv, stat_send, stat_recv, panel_sem,
+):
+    width = BUCKET_WIDTH
+    s = lax.axis_index("sample")
+    y = lax.axis_index("gene")
+    z = lax.axis_index("cohort")
+    x, core = s // 2, s % 2
+    z_hi, z_lo = z // 2, z % 2
+    to_core = {"sample": 2 * x + 1 - core}
+    to_x = {"sample": 2 * (1 - x) + core}
+    to_corner = {"sample": 2 * (1 - x) + 1 - core}
+    to_near = {"cohort": 2 * z_hi + 1 - z_lo}
+    to_far = {"cohort": 2 * (1 - z_hi) + z_lo}
+    to_swap = {"sample": 2 * y + core, "gene": x}
+
+    def panel_copy(i):
+        at = pl.multiple_of(i * width, width)
+        return pltpu.make_async_copy(
+            dosage_ref.at[:, pl.ds(at, width)], panel_ref.at[i], panel_sem.at[i]
+        )
+
+    def fetch(i, carry):
+        panel_copy(i).start()
+        return carry
+
+    def fetched(i, carry):
+        panel_copy(i).wait()
+        return carry
+
+    lax.fori_loop(0, panel_ref.shape[0], fetch, 0)
+
+    barrier = pltpu.get_barrier_semaphore()
+    for peer in (to_core, to_x, to_corner, to_near, to_far):
+        pl.semaphore_signal(barrier, inc=1, device_id=peer)
+
+    @pl.when(x != y)
+    def _():
+        pl.semaphore_signal(barrier, inc=1, device_id=to_swap)
+
+    pl.semaphore_wait(barrier, 5 + (x + y) % 2)
+
+    def remote(source, target, sent, arrived, peer):
+        return pltpu.make_async_remote_copy(
+            src_ref=source, dst_ref=target, send_sem=sent, recv_sem=arrived, device_id=peer
+        )
+
+    def core_copy(i):
+        return remote(give.at[i], take_core.at[i], core_send.at[i], core_recv.at[i], to_core)
+
+    def x_copy(i):
+        return remote(own.at[i], take_x.at[i], x_send.at[i], x_recv.at[i], to_x)
+
+    def near_copy(i):
+        return remote(own.at[8 + i], take_near.at[i], near_send.at[i], near_recv.at[i], to_near)
+
+    def far_copy(i):
+        return remote(own.at[12 + i], take_far.at[i], far_send.at[i], far_recv.at[i], to_far)
+
+    def swap_copy(i):
+        return remote(own.at[14 + i], final.at[i], swap_send.at[i], swap_recv.at[i], to_swap)
+
+    def moment_copy(i):
+        peer = (to_core, to_x, to_near, to_far)[i]
+        return remote(mom_out.at[i], mom_in.at[i], mom_send.at[i], mom_recv.at[i], peer)
+
+    side = side_ref[...]
+    keep = jnp.broadcast_to(side[:, covs + 1 : covs + 2], side.shape)
+    masked_side = side * keep
+    left_t[...] = jnp.transpose(masked_side)[: left_t.shape[0]]
+    mom_out[0] = contract_rows(masked_side, masked_side)[:covs]
+    moment_copy(0).start()
+
+    row, col = square_iota()
+
+    def products(base):
+        panels = []
+        for half in range(2):
+            panels.append(panel_ref[order_ref[base + half]] * keep)
+        first, second = panels
+        gram_a = contract_rows(first, first)
+        gram_b = contract_rows(second, second)
+        left = left_t[...]
+        cross_a = jnp.dot(left, first, preferred_element_type=jnp.float32)
+        cross_b = jnp.dot(left, second, preferred_element_type=jnp.float32)
+        diagonal = jnp.sum(jnp.where(row == col, gram_b, 0.0), axis=0, keepdims=True)
+        last = jnp.concatenate(
+            [
+                cross_a[covs : covs + 1],
+                cross_b[covs : covs + 1],
+                diagonal,
+                jnp.zeros((UNIT - width - 2 * covs - 3, width), jnp.float32),
+            ],
+            axis=0,
+        )
+        return jnp.where(row <= col, gram_a, gram_b), cross_a[:covs], cross_b[:covs], last
+
+    def store_unit(ref, i, base):
+        packed, cross_a, cross_b, last = products(base)
+        ref[i, 0:width] = packed
+        ref[i, width : width + covs] = cross_a
+        ref[i, width + covs : width + 2 * covs] = cross_b
+        ref[i, width + 2 * covs : UNIT] = last
+
+    def table_at(y_to, z_to, core_to, pair):
+        return y * 64 + (y_to * 4 + z_to) * 8 + core_to * 4 + pair * 2
+
+    def produce(i, carry):
+        @pl.when(i < 16)
+        def _():
+            keep_side = i // 8
+            k = (i % 8) // 2
+            pair = i % 2
+            y_to = keep_side * x + (1 - keep_side) * (1 - x)
+            z_to = 2 * ((z_hi + 1 + k) % 2) + (z_lo + 1 + k // 2) % 2
+            store_unit(give, i, table_at(y_to, z_to, 1 - core, pair))
+            core_copy(i).start()
+            store_unit(own, i, table_at(y_to, z_to, core, pair))
+
+        @pl.when((i >= 1) & (i <= 8))
+        def _():
+            core_copy(i - 1).wait_recv()
+            own[i - 1] = own[i - 1] + take_core[i - 1]
+            x_copy(i - 1).start()
+
+        for step in range(3):
+            @pl.when(i == 4 * step + 3)
+            def _():
+                moment_copy(step).wait_recv()
+                mom_out[step + 1] = mom_out[step] + mom_in[step]
+                moment_copy(step + 1).start()
+
+        return carry
+
+    lax.fori_loop(0, panel_ref.shape[0], fetched, 0)
+    lax.fori_loop(0, 16, produce, 0)
+
+    def meet(i):
+        core_copy(8 + i).wait_recv()
+        x_copy(i).wait_recv()
+        return own[8 + i] + take_core[8 + i] + take_x[i]
+
+    def to_neighbour(i, carry):
+        own[8 + i] = meet(i)
+        near_copy(i).start()
+        return carry
+
+    lax.fori_loop(0, 4, to_neighbour, 0)
+
+    moment_copy(3).wait_recv()
+    moments = mom_out[3] + mom_in[3]
+    r = lax.broadcasted_iota(jnp.int32, (covs, width), 0)
+    c = lax.broadcasted_iota(jnp.int32, (covs, width), 1)
+    work = jnp.where(c <= covs, moments, jnp.where(c == r + 64, 1.0, 0.0))
+    for k in range(covs):
+        scale = 1.0 / jnp.sqrt(work[k : k + 1, k : k + 1])
+        pivot = work[k : k + 1, :] * scale
+        below = work[:, k : k + 1] * scale
+        work = jnp.where(r > k, work - below * pivot, jnp.where(r == k, pivot, work))
+    half_score = work[:, covs : covs + 1]
+    inverse = work[:, 64 : 64 + covs]
+
+    def to_far_side(i, carry):
+        part = meet(4 + i)
+        near_copy(i).wait_recv()
+        own[12 + i] = part + take_near[i]
+        far_copy(i).start()
+        return carry
+
+    lax.fori_loop(0, 2, to_far_side, 0)
+
+    for i in range(2):
+        part = meet(6 + i)
+        near_copy(2 + i).wait_recv()
+        far_copy(i).wait_recv()
+        part = part + take_near[2 + i] + take_far[i]
+
+        @pl.when(x == y)
+        def _():
+            final[i] = part
+
+        @pl.when(x != y)
+        def _():
+            own[14 + i] = part
+            swap_copy(i).start()
+
+    owner_base = (y * 4 + z) * GENES_OWN
+    slot_base = x * 64 + (y * 4 + z) * 8 + core * 4
+    squares, sums, traces = [], [], []
+    labels = []
+    for i in range(2):
+        @pl.when(x != y)
+        def _():
+            swap_copy(i).wait_recv()
+
+        packed = final[i, 0:width]
+        mirrored = jnp.transpose(packed)
+        last = final[i, width + 2 * covs : UNIT]
+        gram_b = jnp.where(row > col, packed, jnp.where(row == col, last[2:3], mirrored))
+        grams = (jnp.where(row <= col, packed, mirrored), gram_b)
+        for half in range(2):
+            cross = final[i, width + half * covs : width + (half + 1) * covs]
+            solved = jnp.dot(
+                inverse, cross, precision=lax.Precision.HIGHEST,
+                preferred_element_type=jnp.float32,
+            )
+            projected = lax.dot_general(
+                solved, solved, (((0,), (0,)), ((), ())), precision=lax.Precision.HIGHEST,
+                preferred_element_type=jnp.float32,
+            )
+            bucket = order_ref[slot_base + 2 * i + half] + x * 64
+            label = gene_ref[bucket]
+            live = jnp.where(label >= 0, weight_ref[bucket], 0.0)
+            across = jnp.broadcast_to(live, (width, width))
+            tile = across * jnp.transpose(across) * (grams[half] - projected) / sample_total
+            tile_ref[0, 2 * i + half] = tile
+            score = last[half : half + 1] - jnp.sum(solved * half_score, axis=0, keepdims=True)
+            zscore = live * score / math.sqrt(sample_total)
+            squares.append(zscore * zscore)
+            sums.append(zscore)
+            traces.append(jnp.sum(jnp.where(row == col, tile, 0.0), axis=0, keepdims=True))
+            labels.append(label - owner_base)
+
+    gene_row = lax.broadcasted_iota(jnp.int32, (GENES_OWN, width), 0)
+    gene_col = lax.broadcasted_iota(jnp.int32, (GENES_OWN, width), 1)
+    for n, group in enumerate((squares, sums, traces)):
+        total = jnp.zeros((GENES_OWN, width), jnp.float32)
+        for label, value in zip(labels, group):
+            total = total + jnp.where(label == gene_row, value, 0.0)
+        stats[s, n * GENES_OWN : (n + 1) * GENES_OWN] = total
+
+    def stat_copy(n):
+        peer = (to_core, to_x, to_corner)[n]
+        return remote(stats.at[s], stats.at[s], stat_send.at[n], stat_recv.at[n], peer)
+
+    for n in range(3):
+        stat_copy(n).start()
+    for n in range(3):
+        stat_copy(n).wait_recv()
+
+    def gene_totals(n):
+        at = slice(n * GENES_OWN, (n + 1) * GENES_OWN)
+        lanes = (stats[0, at] + stats[1, at]) + (stats[2, at] + stats[3, at])
+        total = jnp.sum(lanes, axis=1, keepdims=True)
+        return jnp.sum(jnp.where(gene_row == gene_col, total, 0.0), axis=0, keepdims=True)
+
+    square, burden, trace = gene_totals(0), gene_totals(1), gene_totals(2)
+    rho = jnp.zeros((len(RHO_GRID), width), jnp.float32)
+    for n, value in enumerate(RHO_GRID):
+        rho = jnp.where(gene_row == n, value, rho)
+    rho_all = ((1.0 - rho) * square + rho * (burden * burden)) / width
+    rho_ref[...] = rho_all[:, :GENES_OWN]
+    trace_ref[...] = trace[:, :GENES_OWN] / width
+
+    def sent_core(i, carry):
+        core_copy(i).wait_send()
+        return carry
+
+    lax.fori_loop(0, 16, sent_core, 0)
+
+    def sent_x(i, carry):
+        x_copy(i).wait_send()
+        return carry
+
+    lax.fori_loop(0, 8, sent_x, 0)
+    for i in range(4):
+        near_copy(i).wait_send()
+        moment_copy(i).wait_send()
+    for i in range(3):
+        stat_copy(i).wait_send()
+    for i in range(2):
+        far_copy(i).wait_send()
+
+        @pl.when(x != y)
+        def _():
+            swap_copy(i).wait_send()
+
+
+def bucket_order(bucket_owner, gene_count, owner_count):
+    total = bucket_owner.shape[0]
+    bucket = jnp.arange(total, dtype=jnp.int32)
+    block = bucket // (total // gene_count)
+    label = block * owner_count + bucket_owner
+    before = (label[:, None] == label[None, :]) & (bucket[None, :] < bucket[:, None])
+    rank = jnp.sum(before.astype(jnp.int32), axis=1)
+    place = label * (total // (gene_count * owner_count)) + rank
+    inside = bucket % (total // gene_count)
+    return jnp.sum(jnp.where(place[None, :] == bucket[:, None], inside[None, :], 0), axis=1)
+
+
+def shards_fused(
+    dosage, covariates, phenotype, sample_mask, variant_weight, bucket_owner, variant_gene
+):
+    width = BUCKET_WIDTH
+    rows, covs = covariates.shape
+    total = bucket_owner.shape[0]
+    sample_total = rows * lax.axis_size("sample") * lax.axis_size("cohort")
+    order = bucket_order(bucket_owner, 2, 8)
+    side = jnp.concatenate(
+        [
+            covariates,
+            phenotype[:, None],
+            sample_mask.astype(jnp.bfloat16)[:, None],
+            jnp.zeros((rows, width - covs - 2), jnp.bfloat16),
+        ],
+        axis=1,
+    )
+    vmem = pl.BlockSpec(memory_space=pltpu.VMEM)
+
+    def units(count):
+        return pltpu.VMEM((count, UNIT, width), jnp.float32)
+
+    counts = (16, 16, 8, 8, 4, 4, 2, 2, 2, 2, 4, 4, 3, 3)
+    counts = counts + (dosage.shape[1] // width,)
+    sems = [pltpu.SemaphoreType.DMA((count,)) for count in counts]
+    tiles, rho_stats, gene_trace = pl.pallas_call(
+        functools.partial(window_kernel, covs, sample_total),
+        out_shape=(
+            jax.ShapeDtypeStruct((1, 4, width, width), jnp.float32),
+            jax.ShapeDtypeStruct((len(RHO_GRID), GENES_OWN), jnp.float32),
+            jax.ShapeDtypeStruct((1, GENES_OWN), jnp.float32),
+        ),
+        in_specs=[pl.BlockSpec(memory_space=pltpu.SMEM), pl.BlockSpec(memory_space=pl.ANY)]
+        + [vmem] * 3,
+        out_specs=(vmem, vmem, vmem),
+        scratch_shapes=[
+            pltpu.VMEM((dosage.shape[1] // width, rows, width), jnp.bfloat16),
+            pltpu.VMEM((48, rows), jnp.bfloat16),
+            units(16), units(16), units(16), units(8), units(4), units(2), units(2),
+            pltpu.VMEM((4, covs, width), jnp.float32),
+            pltpu.VMEM((4, covs, width), jnp.float32),
+            pltpu.VMEM((4, 3 * GENES_OWN, width), jnp.float32),
+        ] + sems,
+        compiler_params=pltpu.CompilerParams(
+            collective_id=0, has_side_effects=True, vmem_limit_bytes=40 * 1024 * 1024
+        ),
+        cost_estimate=pl.CostEstimate(
+            flops=2 * rows * width * 176 * 64, bytes_accessed=2 * dosage.size, transcendentals=0
+        ),
+    )(
+        order, dosage, side,
+        variant_weight.reshape(total, 1, width), variant_gene.reshape(total, 1, width),
+    )
+    return tiles, rho_stats, gene_trace.reshape(GENES_OWN)
+
+
 def solution(mesh):
     placed = (
         P(("sample", "cohort"), "gene"),
@@ -154,8 +524,11 @@
         P(),
         P(),
     )
+    shape = dict(mesh.shape)
+    fused = (shape["sample"], shape["gene"], shape["cohort"]) == (4, 2, 4)
+    body = shards_fused if fused else shards
     return jax.shard_map(
-        shards,
+        body,
         mesh=mesh,
         in_specs=placed,
         out_specs=(

time: 416 us -> 62 us (0.15)
  blocking collectives: 246 us -> 0 us
  Pallas kernels: 0 us -> 49.7 us
  local copies, waits for them, and re-layouts: 54.4 us -> 8.77 us
  waiting for transfers between devices: 38.1 us -> 0 us
  other arithmetic: 31.2 us -> 2.44 us
  matrix products: 23.8 us -> 0 us
  between operations: 14.3 us -> 0.7 us
  starting transfers between devices: 7.46 us -> 0 us
    all_gather x1 -> x0, blocking collectives: 187 us -> none  [shards(): lax.all_gather(left_cols[:, None, :], 'cohort', axis=1, tiled=True)]
    psum x1 -> x0, blocking collectives: 58.5 us -> none  [shards(): lax.psum(inner_rows(masked_cov, jnp.concatenate([covariates, phenotype[:,...]
    pallas_call x0 -> x1, Pallas kernels: none -> 49.7 us  [shards_fused(): pl.pallas_call(functools.partial(window_kernel, covs, sample_total), out_...]
    psum x1 -> x0, waiting for transfers between devices: 38.1 us -> none  [shards(): gram, cross = lax.psum((gram, cross), 'sample')]
    dot_general x8 -> x0, matrix products: 21.8 us -> none  [the longest x1 9.24 us: shards(): jnp.einsum('schj,schk->hjk', owned, owned, preferred_element_type=jnp.flo...]
    gather x7 -> x0, local copies, waits for them, and re-layouts: 21.4 us -> none  [the longest x1 8.91 us: shards(): jnp.take(arrived, flat_index, axis=1)]
    mul x5 -> x0, other arithmetic: 14.7 us -> none  [the longest x1 7.47 us: shards(): jnp.take(masked_dosage, send_pick, axis=1)]
    reshape x2 -> x0, local copies, waits for them, and re-layouts: 12 us -> none  [the longest x1 11.9 us: shards(): (dosage * sample_keep[:, None]).reshape(sample_rows, src_buckets, span_wi...]
  transfers between devices with their start and end apart: 2 -> 0, of which waited for: 1 -> 0; matrix products, arithmetic and copies ran while one was open for 3% -> 0% of each run, Pallas kernels for 0% -> 0%
where the time goes in v1:
time: 62 us; the launch traced here: 61.6 us
  Pallas kernels  49.7 us (80%)
  local copies, waits for them, and re-layouts  8.77 us (14%)
  other arithmetic  2.44 us (4%)
  between operations  0.7 us (1%)
    pallas_call x1, Pallas kernels, shards_fused(): pl.pallas_call(functools.partial(window_kernel, covs, sample_total), out_...  49.7 us
    unnamed x10, local copies, waits for them, and re-layouts  7.74 us

profile of v1, /device:TPU:0, one launch (start us, length us, event | category | flops | bytes accessed | tf_op | source)
XLA Modules:
  0.0 61.6 jit_solution(14921964303705961976)
XLA Ops:
  0.6 0.7 %fusion.2 = s32[128]{0:T(128)S(1)} fusion(s32[128]{0:T(128)} %param.12), kind=kLoop, calls=%fused_computation.12 | loop fusion | flops 1280 | bytes 1024 | tf_op jit(solution)/shard_map/add | solution.py:453
  1.3 0.2 convert_reduce_fusion
  1.5 0.1 pad.3.clone
  1.6 0.7 %and_select_fusion = (s32[128]{0:T(128)S(1)}, s32[128]{0:T(128)S(1)}) fusion(s32[128]{0:T(128)S(1)} %convert_reduce_fusion, s32[128]{0:T(128)} %param.12), kind=kLoop, calls=%fused_computation.6 | loop fusion | flops 2048 | bytes 2048 | tf_op jit(solution)/shard_map/jit(remainder)/select_n | solution.py:457
  2.2 0.1 select_reduce_fusion.order_ref
  2.3 0.7 %convert_element_type.7 = bf16[512]{0:T(512)(128)(2,1)S(1)} convert(s32[512]{0:T(512)} %param.10) | non-fusion elementwise | flops 512 | bytes 3072 | tf_op jit(solution)/shard_map/convert_element_type | solution.py:473
  3.0 0.1 broadcast_in_dim.34
  3.2 0.9 %copy.14 = bf16[512,32]{1,0:T(8,128)(2,1)S(1)} copy(bf16[512,32]{0,1:T(8,128)(2,1)} %param.8) | data formatting | bytes 65536 | tf_op args[1]
  4.1 0.8 %broadcast_in_dim.33 = bf16[512,1]{1,0:T(8,128)(2,1)S(1)} reshape(bf16[512]{0:T(512)(128)(2,1)} %param.9) | data formatting | bytes 2048 | tf_op jit(solution)/shard_map/broadcast_in_dim | solution.py:472
  4.9 0.1 maximum_maximum_fusion.side_ref
  5.0 0.0 copy-start
  5.0 3.4 %copy-done = bf16[512,8192]{1,0:T(8,128)(2,1)S(1)} copy-done((bf16[512,8192]{1,0:T(8,128)(2,1)S(1)}, bf16[512,8192]{1,0:T(8,128)(2,1)}, u32[]{:S(2)}) %copy-start) | copy-done | bytes 8388632
  8.4 0.0 copy-start.1
  8.4 0.8 %copy-done.1 = f32[16384]{0:T(1024)S(1)} copy-done((f32[16384]{0:T(1024)S(1)}, f32[16384]{0:T(1024)}, u32[]{:S(2)}) %copy-start.1) | copy-done | bytes 65560
  9.2 0.0 copy-start.2
  9.3 0.8 %copy-done.2 = s32[16384]{0:T(1024)S(1)} copy-done((s32[16384]{0:T(1024)S(1)}, s32[16384]{0:T(1024)}, u32[]{:S(2)}) %copy-start.2) | copy-done | bytes 65560
  10.1 49.7 %shard_map.94 = (f32[1,4,128,128]{3,2,1,0:T(8,128)S(1)}, f32[8,8]{1,0:T(8,128)S(1)}, f32[1,8]{1,0:T(1,128)S(1)}) custom-call(s32[128]{0:T(128)S(1)} %select_reduce_fusion.order_ref, bf16[512,8192]{1,0:T(8,128)(2,1)S(1)} %copy-done, bf16[512,128]{1,0:T(8,128)(2,1)S(1)} %maximum_maximum_fusion.side_ref, f32[128,1,128]{2,1,0:T(1,128)S(1)} %bitcast.3, ...), custom_call_target="tpu_custom_call" | custom-call | flops 1476395008 | bytes 8388608 | tf_op jit(solution)/shard_map/pallas_call | solution.py:486
  59.8 0.7 %copy.20 = f32[1,4,128,128]{3,2,1,0:T(8,128)} copy(f32[1,4,128,128]{3,2,1,0:T(8,128)S(1)} %get-tuple-element.14) | data formatting | bytes 524288
  60.5 0.6 copy.21
  61.1 0.5 copy.22
  (1 shorter events, 0.0 us)
Async XLA Ops:
  5.0 3.4 %copy-start = (bf16[512,8192]{1,0:T(8,128)(2,1)S(1)}, bf16[512,8192]{1,0:T(8,128)(2,1)}, u32[]{:S(2)}) copy-start(bf16[512,8192]{1,0:T(8,128)(2,1)} %dosage_ref.1) | copy-start | bytes 25165828
  8.4 0.8 %copy-start.1 = (f32[16384]{0:T(1024)S(1)}, f32[16384]{0:T(1024)}, u32[]{:S(2)}) copy-start(f32[16384]{0:T(1024)} %param.11) | copy-start | bytes 196612
  9.2 0.8 %copy-start.2 = (s32[16384]{0:T(1024)S(1)}, s32[16384]{0:T(1024)}, u32[]{:S(2)}) copy-start(s32[16384]{0:T(1024)} %param.13) | copy-start | bytes 196612

commit v2 on v1

--- a/solution.py
+++ b/solution.py
@@ -150,12 +150,6 @@
 UNIT = 200
 
 
-def contract_rows(first, second):
-    return lax.dot_general(
-        first, second, (((0,), (0,)), ((), ())), preferred_element_type=jnp.float32
-    )
-
-
 def square_iota():
     shape = (BUCKET_WIDTH, BUCKET_WIDTH)
     return (
@@ -165,11 +159,12 @@
 
 
 def window_kernel(
-    covs, sample_total, order_ref, dosage_ref, side_ref, weight_ref, gene_ref,
+    covs, sample_total, order_ref, dosage_ref, cov_ref, pheno_ref, mask_ref, weight_hbm, gene_hbm,
     tile_ref, rho_ref, trace_ref,
-    panel_ref, left_t, own, give, take_core, take_x, take_near, take_far, final, mom_out, mom_in, stats,
+    weight_ref, gene_ref, panel_ref, left_t, keep_ref, solved_ref, own, give, take_core, take_x, take_near, take_far, final, mom_out, mom_in, stats,
     core_send, core_recv, x_send, x_recv, near_send, near_recv, far_send, far_recv,
     swap_send, swap_recv, mom_send, mom_recv, stat_send, stat_recv, panel_sem,
+    table_sem,
 ):
     width = BUCKET_WIDTH
     s = lax.axis_index("sample")
@@ -199,6 +194,10 @@
         return carry
 
     lax.fori_loop(0, panel_ref.shape[0], fetch, 0)
+    weight_copy = pltpu.make_async_copy(weight_hbm, weight_ref, table_sem.at[0])
+    gene_copy = pltpu.make_async_copy(gene_hbm, gene_ref, table_sem.at[1])
+    weight_copy.start()
+    gene_copy.start()
 
     barrier = pltpu.get_barrier_semaphore()
     for peer in (to_core, to_x, to_corner, to_near, to_far):
@@ -234,11 +233,20 @@
         peer = (to_core, to_x, to_near, to_far)[i]
         return remote(mom_out.at[i], mom_in.at[i], mom_send.at[i], mom_recv.at[i], peer)
 
-    side = side_ref[...]
-    keep = jnp.broadcast_to(side[:, covs + 1 : covs + 2], side.shape)
-    masked_side = side * keep
-    left_t[...] = jnp.transpose(masked_side)[: left_t.shape[0]]
-    mom_out[0] = contract_rows(masked_side, masked_side)[:covs]
+    rows = mask_ref.shape[1]
+    keep_ref[...] = jnp.broadcast_to(
+        mask_ref[...].astype(jnp.float32), keep_ref.shape
+    ).astype(jnp.bfloat16)
+    first_row = lax.broadcasted_iota(jnp.int32, (16, rows), 0) == 0
+    outcome = jnp.where(first_row, pheno_ref[...].astype(jnp.float32), 0.0).astype(jnp.bfloat16)
+    plain = jnp.concatenate([cov_ref[...], outcome], axis=0)
+    left_t[...] = plain * keep_ref[: left_t.shape[0]]
+    padded = jnp.concatenate(
+        [plain, jnp.zeros((width - plain.shape[0], rows), jnp.bfloat16)], axis=0
+    )
+    mom_out[0] = lax.dot_general(
+        left_t[...], padded, (((1,), (1,)), ((), ())), preferred_element_type=jnp.float32
+    )[:covs]
     moment_copy(0).start()
 
     row, col = square_iota()
@@ -246,13 +254,16 @@
     def products(base):
         panels = []
         for half in range(2):
-            panels.append(panel_ref[order_ref[base + half]] * keep)
-        first, second = panels
-        gram_a = contract_rows(first, first)
-        gram_b = contract_rows(second, second)
-        left = left_t[...]
-        cross_a = jnp.dot(left, first, preferred_element_type=jnp.float32)
-        cross_b = jnp.dot(left, second, preferred_element_type=jnp.float32)
+            panels.append(panel_ref[order_ref[base + half]])
+        left, masks = left_t[...], keep_ref[...]
+
+        def multiply(panel):
+            stacked = jnp.concatenate([jnp.transpose(panel) * masks, left], axis=0)
+            product = jnp.dot(stacked, panel, preferred_element_type=jnp.float32)
+            return product[:width], product[width:]
+
+        gram_a, cross_a = multiply(panels[0])
+        gram_b, cross_b = multiply(panels[1])
         diagonal = jnp.sum(jnp.where(row == col, gram_b, 0.0), axis=0, keepdims=True)
         last = jnp.concatenate(
             [
@@ -275,6 +286,11 @@
     def table_at(y_to, z_to, core_to, pair):
         return y * 64 + (y_to * 4 + z_to) * 8 + core_to * 4 + pair * 2
 
+    def meet(i):
+        core_copy(8 + i).wait_recv()
+        x_copy(i).wait_recv()
+        return own[8 + i] + take_core[8 + i] + take_x[i]
+
     def produce(i, carry):
         @pl.when(i < 16)
         def _():
@@ -294,42 +310,35 @@
             x_copy(i - 1).start()
 
         for step in range(3):
-            @pl.when(i == 4 * step + 3)
+            @pl.when(i == 2 * step + 1)
             def _():
                 moment_copy(step).wait_recv()
                 mom_out[step + 1] = mom_out[step] + mom_in[step]
                 moment_copy(step + 1).start()
 
+        @pl.when((i >= 9) & (i <= 12))
+        def _():
+            own[i - 1] = meet(i - 9)
+            near_copy(i - 9).start()
+
+        @pl.when(i == 8)
+        def _():
+            moment_copy(3).wait_recv()
+            moments = mom_out[3] + mom_in[3]
+            r = lax.broadcasted_iota(jnp.int32, (covs, width), 0)
+            c = lax.broadcasted_iota(jnp.int32, (covs, width), 1)
+            work = jnp.where(c <= covs, moments, jnp.where(c == r + 64, 1.0, 0.0))
+            for k in range(covs):
+                scale = 1.0 / jnp.sqrt(work[k : k + 1, k : k + 1])
+                pivot = work[k : k + 1, :] * scale
+                below = work[:, k : k + 1] * scale
+                work = jnp.where(r > k, work - below * pivot, jnp.where(r == k, pivot, work))
+            solved_ref[...] = work
+
         return carry
 
     lax.fori_loop(0, panel_ref.shape[0], fetched, 0)
     lax.fori_loop(0, 16, produce, 0)
-
-    def meet(i):
-        core_copy(8 + i).wait_recv()
-        x_copy(i).wait_recv()
-        return own[8 + i] + take_core[8 + i] + take_x[i]
-
-    def to_neighbour(i, carry):
-        own[8 + i] = meet(i)
-        near_copy(i).start()
-        return carry
-
-    lax.fori_loop(0, 4, to_neighbour, 0)
-
-    moment_copy(3).wait_recv()
-    moments = mom_out[3] + mom_in[3]
-    r = lax.broadcasted_iota(jnp.int32, (covs, width), 0)
-    c = lax.broadcasted_iota(jnp.int32, (covs, width), 1)
-    work = jnp.where(c <= covs, moments, jnp.where(c == r + 64, 1.0, 0.0))
-    for k in range(covs):
-        scale = 1.0 / jnp.sqrt(work[k : k + 1, k : k + 1])
-        pivot = work[k : k + 1, :] * scale
-        below = work[:, k : k + 1] * scale
-        work = jnp.where(r > k, work - below * pivot, jnp.where(r == k, pivot, work))
-    half_score = work[:, covs : covs + 1]
-    inverse = work[:, 64 : 64 + covs]
-
     def to_far_side(i, carry):
         part = meet(4 + i)
         near_copy(i).wait_recv()
@@ -354,6 +363,10 @@
             own[14 + i] = part
             swap_copy(i).start()
 
+    half_score = solved_ref[:, covs : covs + 1]
+    inverse = solved_ref[:, 64 : 64 + covs]
+    weight_copy.wait()
+    gene_copy.wait()
     owner_base = (y * 4 + z) * GENES_OWN
     slot_base = x * 64 + (y * 4 + z) * 8 + core * 4
     squares, sums, traces = [], [], []
@@ -466,22 +479,14 @@
     total = bucket_owner.shape[0]
     sample_total = rows * lax.axis_size("sample") * lax.axis_size("cohort")
     order = bucket_order(bucket_owner, 2, 8)
-    side = jnp.concatenate(
-        [
-            covariates,
-            phenotype[:, None],
-            sample_mask.astype(jnp.bfloat16)[:, None],
-            jnp.zeros((rows, width - covs - 2), jnp.bfloat16),
-        ],
-        axis=1,
-    )
     vmem = pl.BlockSpec(memory_space=pltpu.VMEM)
+    hbm = pl.BlockSpec(memory_space=pltpu.HBM)
 
     def units(count):
         return pltpu.VMEM((count, UNIT, width), jnp.float32)
 
     counts = (16, 16, 8, 8, 4, 4, 2, 2, 2, 2, 4, 4, 3, 3)
-    counts = counts + (dosage.shape[1] // width,)
+    counts = counts + (dosage.shape[1] // width, 2)
     sems = [pltpu.SemaphoreType.DMA((count,)) for count in counts]
     tiles, rho_stats, gene_trace = pl.pallas_call(
         functools.partial(window_kernel, covs, sample_total),
@@ -490,12 +495,15 @@
             jax.ShapeDtypeStruct((len(RHO_GRID), GENES_OWN), jnp.float32),
             jax.ShapeDtypeStruct((1, GENES_OWN), jnp.float32),
         ),
-        in_specs=[pl.BlockSpec(memory_space=pltpu.SMEM), pl.BlockSpec(memory_space=pl.ANY)]
-        + [vmem] * 3,
+        in_specs=[pl.BlockSpec(memory_space=pltpu.SMEM), hbm, vmem, vmem, vmem, hbm, hbm],
         out_specs=(vmem, vmem, vmem),
         scratch_shapes=[
+            pltpu.VMEM((total, 1, width), jnp.float32),
+            pltpu.VMEM((total, 1, width), jnp.int32),
             pltpu.VMEM((dosage.shape[1] // width, rows, width), jnp.bfloat16),
             pltpu.VMEM((48, rows), jnp.bfloat16),
+            pltpu.VMEM((width, rows), jnp.bfloat16),
+            pltpu.VMEM((covs, width), jnp.float32),
             units(16), units(16), units(16), units(8), units(4), units(2), units(2),
             pltpu.VMEM((4, covs, width), jnp.float32),
             pltpu.VMEM((4, covs, width), jnp.float32),
@@ -508,7 +516,7 @@
             flops=2 * rows * width * 176 * 64, bytes_accessed=2 * dosage.size, transcendentals=0
         ),
     )(
-        order, dosage, side,
+        order, dosage, covariates.T, phenotype.reshape(1, rows), sample_mask.reshape(1, rows),
         variant_weight.reshape(total, 1, width), variant_gene.reshape(total, 1, width),
     )
     return tiles, rho_stats, gene_trace.reshape(GENES_OWN)

time: 62 us -> 61.7 us (level)
  other arithmetic: 2.44 us -> 1.61 us
    broadcast_in_dim x3 -> x0, local copies, waits for them, and re-layouts: 0.95 us -> none  [the longest x1 0.81 us: shards_fused(): phenotype[:, None]]
    convert_element_type x1 -> x0, other arithmetic: 0.69 us -> none  [shards_fused(): sample_mask.astype(jnp.bfloat16)[:, None]]
    reshape x0 -> x1, local copies, waits for them, and re-layouts: none -> 0.69 us  [shards_fused(): phenotype.reshape(1, rows)]
    unnamed x10 -> x13, local copies, waits for them, and re-layouts: 7.74 us -> 8.31 us
where the time goes in v2:
time: 61.7 us; the launch traced here: 61.4 us
  Pallas kernels  50.1 us (81%)
  local copies, waits for them, and re-layouts  9 us (15%)
  other arithmetic  1.61 us (3%)
  between operations  0.65 us (1%)
    pallas_call x1, Pallas kernels, shards_fused(): pl.pallas_call(functools.partial(window_kernel, covs, sample_total), out_...  50.1 us
    unnamed x13, local copies, waits for them, and re-layouts  8.31 us

profile of v2, /device:TPU:0, one launch (start us, length us, event | category | flops | bytes accessed | tf_op | source)
XLA Modules:
  0.0 61.4 jit_solution(5810829449352693897)
XLA Ops:
  0.6 0.7 %fusion.2 = s32[128]{0:T(128)S(1)} fusion(s32[128]{0:T(128)} %param.12), kind=kLoop, calls=%fused_computation.11 | loop fusion | flops 1280 | bytes 1024 | tf_op jit(solution)/shard_map/add | solution.py:466
  1.3 0.2 convert_reduce_fusion
  1.5 0.7 %and_select_fusion = (s32[128]{0:T(128)S(1)}, s32[128]{0:T(128)S(1)}) fusion(s32[128]{0:T(128)S(1)} %convert_reduce_fusion, s32[128]{0:T(128)} %param.12), kind=kLoop, calls=%fused_computation.5 | loop fusion | flops 2048 | bytes 2048 | tf_op jit(solution)/shard_map/jit(remainder)/select_n | solution.py:470
  2.1 0.1 select_reduce_fusion.order_ref
  2.2 0.7 %reshape.33.pheno_ref = bf16[1,512]{1,0:T(2,128)(2,1)S(1)} reshape(bf16[512]{0:T(512)(128)(2,1)} %param.9) | data formatting | bytes 2048 | tf_op jit(solution)/shard_map/reshape | solution.py:519
  2.9 0.0 copy-start
  2.9 3.4 %copy-done = bf16[512,8192]{1,0:T(8,128)(2,1)S(1)} copy-done((bf16[512,8192]{1,0:T(8,128)(2,1)S(1)}, bf16[512,8192]{1,0:T(8,128)(2,1)}, u32[]{:S(2)}) %copy-start) | copy-done | bytes 8388632
  6.3 0.0 copy-start.1
  6.3 0.8 %copy-done.1 = f32[16384]{0:T(1024)S(1)} copy-done((f32[16384]{0:T(1024)S(1)}, f32[16384]{0:T(1024)}, u32[]{:S(2)}) %copy-start.1) | copy-done | bytes 65560
  7.2 0.0 copy-start.2
  7.2 0.8 %copy-done.2 = s32[16384]{0:T(1024)S(1)} copy-done((s32[16384]{0:T(1024)S(1)}, s32[16384]{0:T(1024)}, u32[]{:S(2)}) %copy-start.2) | copy-done | bytes 65560
  8.0 0.0 copy-start.3
  8.0 0.8 %copy-done.3 = bf16[512,32]{0,1:T(8,128)(2,1)S(1)} copy-done((bf16[512,32]{0,1:T(8,128)(2,1)S(1)}, bf16[512,32]{0,1:T(8,128)(2,1)}, u32[]{:S(2)}) %copy-start.3) | copy-done | bytes 32792
  8.8 0.0 copy-start.4
  8.8 0.7 %copy-done.4 = s32[512]{0:T(512)S(1)} copy-done((s32[512]{0:T(512)S(1)}, s32[512]{0:T(512)}, u32[]{:S(2)}) %copy-start.4) | copy-done | bytes 2072
  9.4 50.1 %shard_map.94 = (f32[1,4,128,128]{3,2,1,0:T(8,128)S(1)}, f32[8,8]{1,0:T(8,128)S(1)}, f32[1,8]{1,0:T(1,128)S(1)}) custom-call(s32[128]{0:T(128)S(1)} %select_reduce_fusion.order_ref, bf16[512,8192]{1,0:T(8,128)(2,1)S(1)} %copy-done, bf16[32,512]{1,0:T(8,128)(2,1)S(1)} %bitcast.7, bf16[1,512]{1,0:T(2,128)(2,1)S(1)} %reshape.33.pheno_ref, ...), custom_call_target="tpu_custom_call" | custom-call | flops 1476395008 | bytes 8388608 | tf_op jit(solution)/shard_map/pallas_call | solution.py:491
  59.5 0.7 %copy.13 = f32[1,4,128,128]{3,2,1,0:T(8,128)} copy(f32[1,4,128,128]{3,2,1,0:T(8,128)S(1)} %get-tuple-element.14) | data formatting | bytes 524288
  60.3 0.6 copy.14
  60.8 0.5 copy.15
Async XLA Ops:
  2.9 3.4 %copy-start = (bf16[512,8192]{1,0:T(8,128)(2,1)S(1)}, bf16[512,8192]{1,0:T(8,128)(2,1)}, u32[]{:S(2)}) copy-start(bf16[512,8192]{1,0:T(8,128)(2,1)} %dosage_ref.1) | copy-start | bytes 25165828
  6.3 0.8 %copy-start.1 = (f32[16384]{0:T(1024)S(1)}, f32[16384]{0:T(1024)}, u32[]{:S(2)}) copy-start(f32[16384]{0:T(1024)} %param.11) | copy-start | bytes 196612
  7.2 0.8 %copy-start.2 = (s32[16384]{0:T(1024)S(1)}, s32[16384]{0:T(1024)}, u32[]{:S(2)}) copy-start(s32[16384]{0:T(1024)} %param.13) | copy-start | bytes 196612
  8.0 0.8 %copy-start.3 = (bf16[512,32]{0,1:T(8,128)(2,1)S(1)}, bf16[512,32]{0,1:T(8,128)(2,1)}, u32[]{:S(2)}) copy-start(bf16[512,32]{0,1:T(8,128)(2,1)} %param.8) | copy-start | bytes 98308
  8.8 0.7 %copy-start.4 = (s32[512]{0:T(512)S(1)}, s32[512]{0:T(512)}, u32[]{:S(2)}) copy-start(s32[512]{0:T(512)} %param.10) | copy-start | bytes 6148

commit v3 on v2

--- a/solution.py
+++ b/solution.py
@@ -510,7 +510,7 @@
             pltpu.VMEM((4, 3 * GENES_OWN, width), jnp.float32),
         ] + sems,
         compiler_params=pltpu.CompilerParams(
-            collective_id=0, has_side_effects=True, vmem_limit_bytes=40 * 1024 * 1024
+            collective_id=0, has_side_effects=True, vmem_limit_bytes=62 * 1024 * 1024
         ),
         cost_estimate=pl.CostEstimate(
             flops=2 * rows * width * 176 * 64, bytes_accessed=2 * dosage.size, transcendentals=0

time: 61.7 us -> 57.4 us (0.930)
  local copies, waits for them, and re-layouts: 9 us -> 5.32 us
  Pallas kernels: 50.1 us -> 49 us
    unnamed x13 -> x3, local copies, waits for them, and re-layouts: 8.31 us -> 4.07 us
    pallas_call x1, Pallas kernels: 50.1 us -> 49 us  [shards_fused(): pl.pallas_call(functools.partial(window_kernel, covs, sample_total), out_...]
where the time goes in v3:
time: 57.4 us; the launch traced here: 57.1 us
  Pallas kernels  49 us (85%)
  local copies, waits for them, and re-layouts  5.32 us (9%)
  other arithmetic  2.13 us (4%)
  between operations  0.65 us (1%)
    pallas_call x1, Pallas kernels, shards_fused(): pl.pallas_call(functools.partial(window_kernel, covs, sample_total), out_...  49 us
    unnamed x3, local copies, waits for them, and re-layouts  4.07 us
    reshape x1, local copies, waits for them, and re-layouts, shards_fused(): phenotype.reshape(1, rows)  1.26 us

profile of v3, /device:TPU:0, one launch (start us, length us, event | category | flops | bytes accessed | tf_op | source)
XLA Modules:
  0.0 57.1 jit_solution(12165555563817098149)
XLA Ops:
  0.6 0.7 %fusion.2 = s32[128]{0:T(128)S(1)} fusion(s32[128]{0:T(128)} %param.12), kind=kLoop, calls=%fused_computation.11 | loop fusion | flops 1280 | bytes 1024 | tf_op jit(solution)/shard_map/add | solution.py:466
  1.3 0.2 convert_reduce_fusion
  1.5 0.7 %and_select_fusion = (s32[128]{0:T(128)S(1)}, s32[128]{0:T(128)S(1)}) fusion(s32[128]{0:T(128)S(1)} %convert_reduce_fusion, s32[128]{0:T(128)} %param.12), kind=kLoop, calls=%fused_computation.5 | loop fusion | flops 2048 | bytes 2048 | tf_op jit(solution)/shard_map/jit(remainder)/select_n | solution.py:470
  2.1 0.6 %select_reduce_fusion.order_ref = s32[128]{0:T(128)} fusion(s32[128]{0:T(128)S(1)} %get-tuple-element.9, s32[128]{0:T(128)S(1)} %get-tuple-element.10), kind=kLoop, calls=%fused_computation | loop fusion | flops 49024 | bytes 1536 | tf_op jit(solution)/shard_map/reduce_sum | solution.py:471
  2.8 1.3 %reshape.33.pheno_ref = bf16[1,512]{1,0:T(2,128)(2,1)} reshape(bf16[512]{0:T(512)(128)(2,1)} %param.9) | data formatting | bytes 2048 | tf_op jit(solution)/shard_map/reshape | solution.py:519
  4.0 49.0 %shard_map.94 = (f32[1,4,128,128]{3,2,1,0:T(8,128)}, f32[8,8]{1,0:T(8,128)}, f32[1,8]{1,0:T(1,128)}) custom-call(s32[128]{0:T(128)} %select_reduce_fusion.order_ref, bf16[512,8192]{1,0:T(8,128)(2,1)} %dosage_ref.1, bf16[32,512]{1,0:T(8,128)(2,1)} %bitcast.7, bf16[1,512]{1,0:T(2,128)(2,1)} %reshape.33.pheno_ref, s32[1,512]{1,0:T(1,128)} %bitcast.8, ...), custom_call_target="tpu_custom_call" | custom-call | flops 1476395008 | bytes 8388608 | tf_op jit(solution)/shard_map/pallas_call | solution.py:491
  53.0 1.7 %copy.13 = f32[1,4,128,128]{3,2,1,0:T(8,128)} copy(f32[1,4,128,128]{3,2,1,0:T(8,128)} %get-tuple-element.14) | data formatting | bytes 524288
  54.7 1.3 %copy.14 = f32[8,8]{1,0:T(8,128)} copy(f32[8,8]{1,0:T(8,128)} %get-tuple-element.15) | data formatting | bytes 512
  56.0 1.1 %copy.15 = f32[8]{0:T(128)} copy(f32[8]{0:T(128)} %bitcast.9) | data formatting | bytes 64

commit v4 on v3

--- a/solution.py
+++ b/solution.py
@@ -291,6 +291,21 @@
         x_copy(i).wait_recv()
         return own[8 + i] + take_core[8 + i] + take_x[i]
 
+    def close(i):
+        part = meet(6 + i)
+        near_copy(2 + i).wait_recv()
+        far_copy(i).wait_recv()
+        part = part + take_near[2 + i] + take_far[i]
+
+        @pl.when(x == y)
+        def _():
+            final[i] = part
+
+        @pl.when(x != y)
+        def _():
+            own[14 + i] = part
+            swap_copy(i).start()
+
     def produce(i, carry):
         @pl.when(i < 16)
         def _():
@@ -321,48 +336,33 @@
             own[i - 1] = meet(i - 9)
             near_copy(i - 9).start()
 
-        @pl.when(i == 8)
-        def _():
-            moment_copy(3).wait_recv()
-            moments = mom_out[3] + mom_in[3]
-            r = lax.broadcasted_iota(jnp.int32, (covs, width), 0)
-            c = lax.broadcasted_iota(jnp.int32, (covs, width), 1)
-            work = jnp.where(c <= covs, moments, jnp.where(c == r + 64, 1.0, 0.0))
-            for k in range(covs):
-                scale = 1.0 / jnp.sqrt(work[k : k + 1, k : k + 1])
-                pivot = work[k : k + 1, :] * scale
-                below = work[:, k : k + 1] * scale
-                work = jnp.where(r > k, work - below * pivot, jnp.where(r == k, pivot, work))
-            solved_ref[...] = work
+        @pl.when((i >= 13) & (i <= 14))
+        def _():
+            part = meet(i - 9)
+            near_copy(i - 13).wait_recv()
+            own[i - 1] = part + take_near[i - 13]
+            far_copy(i - 13).start()
+
+        @pl.when(i == 15)
+        def _():
+            close(0)
 
         return carry
 
     lax.fori_loop(0, panel_ref.shape[0], fetched, 0)
     lax.fori_loop(0, 16, produce, 0)
-    def to_far_side(i, carry):
-        part = meet(4 + i)
-        near_copy(i).wait_recv()
-        own[12 + i] = part + take_near[i]
-        far_copy(i).start()
-        return carry
-
-    lax.fori_loop(0, 2, to_far_side, 0)
-
-    for i in range(2):
-        part = meet(6 + i)
-        near_copy(2 + i).wait_recv()
-        far_copy(i).wait_recv()
-        part = part + take_near[2 + i] + take_far[i]
-
-        @pl.when(x == y)
-        def _():
-            final[i] = part
-
-        @pl.when(x != y)
-        def _():
-            own[14 + i] = part
-            swap_copy(i).start()
-
+    close(1)
+    moment_copy(3).wait_recv()
+    moments = mom_out[3] + mom_in[3]
+    r = lax.broadcasted_iota(jnp.int32, (covs, width), 0)
+    c = lax.broadcasted_iota(jnp.int32, (covs, width), 1)
+    work = jnp.where(c <= covs, moments, jnp.where(c == r + 64, 1.0, 0.0))
+    for k in range(covs):
+        scale = 1.0 / jnp.sqrt(work[k : k + 1, k : k + 1])
+        pivot = work[k : k + 1, :] * scale
+        below = work[:, k : k + 1] * scale
+        work = jnp.where(r > k, work - below * pivot, jnp.where(r == k, pivot, work))
+    solved_ref[...] = work
     half_score = solved_ref[:, covs : covs + 1]
     inverse = solved_ref[:, 64 : 64 + covs]
     weight_copy.wait()

time: 57.4 us -> 52.5 us (0.915)
  Pallas kernels: 49 us -> 44.1 us
    pallas_call x1, Pallas kernels: 49 us -> 44.1 us  [shards_fused(): pl.pallas_call(functools.partial(window_kernel, covs, sample_total), out_...]
where the time goes in v4:
time: 52.5 us; the launch traced here: 52.2 us
  Pallas kernels  44.1 us (84%)
  local copies, waits for them, and re-layouts  5.32 us (10%)
  other arithmetic  2.13 us (4%)
  between operations  0.65 us (1%)
    pallas_call x1, Pallas kernels, shards_fused(): pl.pallas_call(functools.partial(window_kernel, covs, sample_total), out_...  44.1 us
    unnamed x3, local copies, waits for them, and re-layouts  4.07 us
    reshape x1, local copies, waits for them, and re-layouts, shards_fused(): phenotype.reshape(1, rows)  1.26 us

profile of v4, /device:TPU:0, one launch (start us, length us, event | category | flops | bytes accessed | tf_op | source)
XLA Modules:
  0.0 52.2 jit_solution(16915232043945383701)
XLA Ops:
  0.6 0.7 %fusion.2 = s32[128]{0:T(128)S(1)} fusion(s32[128]{0:T(128)} %param.12), kind=kLoop, calls=%fused_computation.11 | loop fusion | flops 1280 | bytes 1024 | tf_op jit(solution)/shard_map/add | solution.py:466
  1.3 0.2 convert_reduce_fusion
  1.5 0.7 %and_select_fusion = (s32[128]{0:T(128)S(1)}, s32[128]{0:T(128)S(1)}) fusion(s32[128]{0:T(128)S(1)} %convert_reduce_fusion, s32[128]{0:T(128)} %param.12), kind=kLoop, calls=%fused_computation.5 | loop fusion | flops 2048 | bytes 2048 | tf_op jit(solution)/shard_map/jit(remainder)/select_n | solution.py:470
  2.1 0.6 %select_reduce_fusion.order_ref = s32[128]{0:T(128)} fusion(s32[128]{0:T(128)S(1)} %get-tuple-element.9, s32[128]{0:T(128)S(1)} %get-tuple-element.10), kind=kLoop, calls=%fused_computation | loop fusion | flops 49024 | bytes 1536 | tf_op jit(solution)/shard_map/reduce_sum | solution.py:471
  2.8 1.3 %reshape.33.pheno_ref = bf16[1,512]{1,0:T(2,128)(2,1)} reshape(bf16[512]{0:T(512)(128)(2,1)} %param.9) | data formatting | bytes 2048 | tf_op jit(solution)/shard_map/reshape | solution.py:519
  4.0 44.1 %shard_map.94 = (f32[1,4,128,128]{3,2,1,0:T(8,128)}, f32[8,8]{1,0:T(8,128)}, f32[1,8]{1,0:T(1,128)}) custom-call(s32[128]{0:T(128)} %select_reduce_fusion.order_ref, bf16[512,8192]{1,0:T(8,128)(2,1)} %dosage_ref.1, bf16[32,512]{1,0:T(8,128)(2,1)} %bitcast.7, bf16[1,512]{1,0:T(2,128)(2,1)} %reshape.33.pheno_ref, s32[1,512]{1,0:T(1,128)} %bitcast.8, ...), custom_call_target="tpu_custom_call" | custom-call | flops 1476395008 | bytes 8388608 | tf_op jit(solution)/shard_map/pallas_call | solution.py:491
  48.1 1.7 %copy.13 = f32[1,4,128,128]{3,2,1,0:T(8,128)} copy(f32[1,4,128,128]{3,2,1,0:T(8,128)} %get-tuple-element.14) | data formatting | bytes 524288
  49.8 1.3 %copy.14 = f32[8,8]{1,0:T(8,128)} copy(f32[8,8]{1,0:T(8,128)} %get-tuple-element.15) | data formatting | bytes 512
  51.0 1.1 %copy.15 = f32[8]{0:T(128)} copy(f32[8]{0:T(128)} %bitcast.9) | data formatting | bytes 64
